TPU v7x, 32 devices: a whole 2x2x4 slice. The times are simulated.
32 devices in a mesh: section: 2 (over core), req: 4 (over y, x), head: 4 (over z).
Axes of the slice: x: 2, y: 2, z: 4, core: 2. Of those that a mesh axis runs over, the one named last changes fastest.
Arguments:
- tokens: bfloat16 [64, 8192], P(None, 'req'), may hold values from -14 to 14
- attention_gain: bfloat16 [2, 8192], P('section', 'req'), may hold values from 0.099609375 to 1.8984375
- query_key_value_weight: bfloat16 [2, 8192, 8, 1280], P('section', 'req', 'head'), may hold values from -0.0625 to 0.0625
- head_output_weight: bfloat16 [2, 8, 1024, 8192], P('section', 'head', None, 'req'), may hold values from -0.0625 to 0.0625
- feedforward_gain: bfloat16 [2, 8192], P('section', 'req'), may hold values from 0.099609375 to 1.8984375
- gate_up: bfloat16 [2, 8192, 2, 14336], P('section', 'req', None, 'head'), may hold values from -0.0625 to 0.0625
- down_weight: bfloat16 [2, 14336, 8192], P('section', 'head', 'req'), may hold values from -0.046875 to 0.046875
- packed_cache: bfloat16 [2, 8192, 8, 256], P('section', 'req', 'head'), may hold values from -70 to 70
- long_cache: bfloat16 [2, 2, 32768, 8, 256], P('section', None, 'req', 'head'), may hold values from -70 to 70
- lengths: int32 [4, 16], P('req'), may hold values from 1 to 256, 2048 in all within a row
- long_split: int32 [2, 4], P(None, 'req'), may hold values from 1 to 8192, 16384 in all within a row
Outputs:
- layer_outputs: bfloat16 [2, 64, 8192], P('section', None, 'req')
Inputs may be any that keep to these rules, and one draw needn't show every extreme that they name: Row g holds the lengths of the 16 requests of request group g in order; they sum to 2048, and the requests' keys fill that group's 2048 slots of packed_cache one request after another. `long_split`: entry (j, g) counts the live slots, the first ones, of group g's 8192 slots of long request j; each row sums to 16384.
All inputs are finite; a program needn't handle non-finite values.
Results may differ from a plain program's by a relative error of at most 0.04.
Values may be sent and summed in bfloat16 or wider, within the bound.
No kernel may reach another device: no remote copies, remote signals or barrier semaphores. Data moves between devices by JAX's collectives and lax.ppermute only.
A program may use at most 192 MiB of HBM per device.

v0:
```python
import math

import jax
import jax.numpy as jnp
from jax import lax
from jax.sharding import PartitionSpec as P

MODEL_WIDTH = 8192
QUERY_HEADS = 64
KEY_VALUE_HEADS = 8
HEAD_SIZE = 128
LONG = 16384


EPSILON = 1e-05


def merged(part, axis, combine):
    gathered = jax.tree.map(lambda a: lax.all_gather(a, axis), part)

    def take(source):
        return jax.tree.map(lambda a: lax.dynamic_index_in_dim(a, source, 0, False), gathered)

    return lax.fori_loop(
        1, lax.axis_size(axis), lambda source, state: combine(state, take(source)), take(0)
    )


def shifted(value, axis, by):
    peers = lax.axis_size(axis)
    pairs = [(i, i + by) for i in range(peers) if 0 <= i + by < peers]
    return lax.ppermute(value, axis, pairs)


def rotate(values, position):
    half_dim = values.shape[-1] // 2
    freq_ids = jnp.arange(half_dim).astype(jnp.float32)
    inverse = 1.0 / 10000.0 ** (freq_ids * 2.0 / values.shape[-1])
    angles = position.astype(jnp.float32)[:, None] * inverse[None, :]
    cosine = jnp.cos(angles)[:, None, None, :]
    sine_part = jnp.sin(angles)[:, None, None, :]
    lower_half = values[..., :half_dim]
    upper_half = values[..., half_dim:]
    return jnp.concatenate(
        [
            lower_half * cosine - upper_half * sine_part,
            upper_half * cosine + lower_half * sine_part,
        ],
        -1,
    )


def add_pair(earlier, second_part):
    return earlier + second_part


def combine_partial(earlier, second_part):
    peak = jnp.maximum(earlier[0], second_part[0])
    left_factor = jnp.exp(earlier[0] - peak)
    right_factor = jnp.exp(second_part[0] - peak)
    softmax_total = earlier[1] * left_factor + second_part[1] * right_factor
    weighted_sum = earlier[2] * left_factor[..., None] + second_part[2] * right_factor[..., None]
    return (peak, softmax_total, weighted_sum)


def over_requests(values, combiner):
    return merged(values, "req", combiner)


def rows_apply(values, row_fn):
    return row_fn(lax.all_gather(values, "req", axis=0, tiled=True), jnp.int32(0))


def rows_project(term_fn, row_count):
    return lax.psum_scatter(
        term_fn(jnp.int32(0), row_count * lax.axis_size("req")),
        "req",
        scatter_dimension=0,
        tiled=True,
    )


def head_total(values):
    return lax.psum(values, "head")


def keep_rows(piece_rows, start_row):
    return piece_rows


def norm_rows(values, gain_row):
    floats = values.astype(jnp.float32)
    squares = over_requests(jnp.sum(floats * floats, axis=-1), add_pair)
    return (
        floats * lax.rsqrt(squares / MODEL_WIDTH + EPSILON)[:, None] * gain_row.astype(jnp.float32)
    ).astype(jnp.bfloat16)


def decoder_layer(
    inputs,
    micro_batch,
    attention_gain,
    query_key_value_weight,
    head_output_weight,
    feedforward_gain,
    gate_up,
    down_weight,
    packed_cache,
    long_cache,
    lengths,
    long_split,
):
    req_count = lax.axis_size("req")
    group_index = lax.axis_index("req")
    blocks = inputs.shape[0] // req_count
    columns = query_key_value_weight.shape[1]
    kv_local = query_key_value_weight.shape[2]
    requests_per_group = QUERY_HEADS // KEY_VALUE_HEADS
    score_scale = 1.0 / math.sqrt(HEAD_SIZE)
    normalized_input = norm_rows(inputs, attention_gain[0])
    in_weights = query_key_value_weight[0].reshape(
        columns, kv_local * (requests_per_group + 2) * HEAD_SIZE
    )

    def qkv_term(start_row, row_count):
        return jnp.dot(normalized_input, in_weights, preferred_element_type=jnp.float32)

    projected_rows = rows_project(qkv_term, blocks).reshape(
        blocks, kv_local, requests_per_group + 2, HEAD_SIZE
    )
    local_rows = jnp.arange(blocks)
    row_lengths = lengths[0]
    owner_long = (group_index == 0) | (group_index == req_count // 2)
    long_row = (local_rows == 0) & (micro_batch == 0) & owner_long
    position = row_lengths + jnp.where(long_row, LONG, 0).astype(jnp.int32)
    queries = rotate(projected_rows[:, :, :requests_per_group], position).astype(jnp.bfloat16)
    new_key = rotate(projected_rows[:, :, requests_per_group : requests_per_group + 1], position)[
        :, :, 0
    ].astype(jnp.bfloat16)
    new_value = projected_rows[:, :, requests_per_group + 1].astype(jnp.bfloat16)
    gathered = rows_apply(
        queries[0:1].reshape(1, kv_local * requests_per_group * HEAD_SIZE), keep_rows
    )
    long_queries = jnp.stack([gathered[0], gathered[req_count // 2]]).reshape(
        2, kv_local, requests_per_group, HEAD_SIZE
    )
    far_cache = long_cache[0]
    far_live = (jnp.arange(far_cache.shape[1])[None, :] < long_split[:, 0][:, None])[
        :, None, None, :
    ]
    far_scores = (
        jnp.einsum(
            "jkhd,jpkd->jkhp",
            long_queries,
            far_cache[..., :HEAD_SIZE],
            preferred_element_type=jnp.float32,
        )
        * score_scale
    )
    far_max = jnp.max(jnp.where(far_live, far_scores, -jnp.inf), axis=-1)
    far_weights = jnp.where(
        far_live, jnp.exp(jnp.where(far_live, far_scores - far_max[..., None], 0.0)), 0.0
    ).astype(jnp.bfloat16)
    far_totals = jnp.sum(far_weights.astype(jnp.float32), axis=-1)
    far_summed = jnp.einsum(
        "jkhp,jpkd->jkhd",
        far_weights,
        far_cache[..., HEAD_SIZE:],
        preferred_element_type=jnp.float32,
    )
    far_max, far_totals, far_summed = over_requests(
        (far_max, far_totals, far_summed), combine_partial
    )
    far_index = jnp.where(group_index == 0, 0, 1)
    chosen_max = lax.dynamic_index_in_dim(far_max, far_index, 0, keepdims=False)
    chosen_totals = lax.dynamic_index_in_dim(far_totals, far_index, 0, keepdims=False)
    chosen_summed = lax.dynamic_index_in_dim(far_summed, far_index, 0, keepdims=False)
    pack_part = packed_cache[0]
    seg_ends = jnp.cumsum(lengths[0])
    slot_ids = jnp.arange(pack_part.shape[0])
    slot_owner = jnp.sum((slot_ids[:, None] >= seg_ends[None, :]).astype(jnp.int32), axis=1)
    request_ids = micro_batch * blocks + local_rows
    in_segment = (slot_owner[None, :] == request_ids[:, None])[:, None, None, :]
    scores = (
        jnp.einsum(
            "rkhd,pkd->rkhp",
            queries,
            pack_part[..., :HEAD_SIZE],
            preferred_element_type=jnp.float32,
        )
        * score_scale
    )
    own_score = (
        jnp.einsum("rkhd,rkd->rkh", queries, new_key, preferred_element_type=jnp.float32)
        * score_scale
    )
    row_max = jnp.maximum(jnp.max(jnp.where(in_segment, scores, -jnp.inf), axis=-1), own_score)
    long_mask = long_row[:, None, None]
    row_max = jnp.where(long_mask, jnp.maximum(row_max, chosen_max[None]), row_max)
    weights = jnp.where(
        in_segment, jnp.exp(jnp.where(in_segment, scores - row_max[..., None], 0.0)), 0.0
    ).astype(jnp.bfloat16)
    own_weights = jnp.exp(own_score - row_max).astype(jnp.bfloat16)
    far_factor = jnp.where(
        long_mask, jnp.exp(jnp.where(long_mask, chosen_max[None] - row_max, 0.0)), 0.0
    )
    softmax_total = (
        jnp.sum(weights.astype(jnp.float32), axis=-1)
        + own_weights.astype(jnp.float32)
        + far_factor * chosen_totals[None]
    )
    weighted_sum = jnp.einsum(
        "rkhp,pkd->rkhd", weights, pack_part[..., HEAD_SIZE:], preferred_element_type=jnp.float32
    )
    weighted_sum = (
        weighted_sum
        + own_weights.astype(jnp.float32)[..., None] * new_value.astype(jnp.float32)[:, :, None, :]
    )
    weighted_sum = weighted_sum + far_factor[..., None] * chosen_summed[None]
    attended_heads = (
        (weighted_sum / softmax_total[..., None])
        .astype(jnp.bfloat16)
        .reshape(blocks, kv_local * requests_per_group * HEAD_SIZE)
    )
    out_weights = head_output_weight[0].reshape(kv_local * requests_per_group * HEAD_SIZE, columns)

    def project_heads(piece_rows, start_row):
        return jnp.dot(piece_rows, out_weights, preferred_element_type=jnp.float32)

    attended = head_total(rows_apply(attended_heads, project_heads))
    residual = (inputs.astype(jnp.float32) + attended).astype(jnp.bfloat16)
    normed_two = norm_rows(residual, feedforward_gain[0])
    ff_weights = gate_up[0].reshape(columns, -1)

    def ff_term(start_row, row_count):
        return jnp.dot(normed_two, ff_weights, preferred_element_type=jnp.float32)

    gate_and_up = rows_project(ff_term, blocks)
    hidden_width = gate_and_up.shape[1] // 2
    hidden = (jax.nn.silu(gate_and_up[:, :hidden_width]) * gate_and_up[:, hidden_width:]).astype(
        jnp.bfloat16
    )
    lower_weights = down_weight[0]

    def project_hidden(piece_rows, start_row):
        return jnp.dot(piece_rows, lower_weights, preferred_element_type=jnp.float32)

    lowered = head_total(rows_apply(hidden, project_hidden))
    return (residual.astype(jnp.float32) + lowered).astype(jnp.bfloat16)


def local(
    tokens,
    attention_gain,
    query_key_value_weight,
    head_output_weight,
    feedforward_gain,
    gate_up,
    down_weight,
    packed_cache,
    long_cache,
    lengths,
    long_split,
):
    req_count = lax.axis_size("req")
    section_index = lax.axis_index("section")
    batch_count = 1
    per_group = tokens.shape[0] // req_count
    blocks = per_group // batch_count
    columns = tokens.shape[1]
    token_grid = tokens.reshape(req_count, per_group, columns)
    result = jnp.zeros_like(token_grid)
    incoming = jnp.zeros((req_count * blocks, columns), jnp.bfloat16)
    for phase_step in range(batch_count + 1):
        micro_batch = phase_step - section_index
        is_active = (micro_batch >= 0) & (micro_batch < batch_count)
        micro_batch = jnp.clip(micro_batch, 0, batch_count - 1)
        new_batch = token_grid.reshape(req_count * blocks, columns)
        inputs = jnp.where(section_index == 0, new_batch, incoming)
        output = decoder_layer(
            inputs,
            micro_batch,
            attention_gain,
            query_key_value_weight,
            head_output_weight,
            feedforward_gain,
            gate_up,
            down_weight,
            packed_cache,
            long_cache,
            lengths,
            long_split,
        )
        placed = output.reshape(req_count, blocks, columns)
        result = jnp.where(is_active, placed, result)
        if phase_step < batch_count:
            incoming = shifted(output, "section", 1)
    return result.reshape(1, req_count * per_group, columns)


def solution(mesh):
    placed = (
        P(None, "req"),
        P("section", "req"),
        P("section", "req", "head", None),
        P("section", "head", None, "req"),
        P("section", "req"),
        P("section", "req", None, "head"),
        P("section", "head", "req"),
        P("section", "req", "head", None),
        P("section", None, "req", "head", None),
        P("req", None),
        P(None, "req"),
    )
    return jax.shard_map(
        local, mesh=mesh, in_specs=placed, out_specs=P("section", None, "req"), check_vma=False
    )
```

profile of v0, /device:TPU:1, one launch (start us, length us, event | category | flops | bytes accessed | tf_op | source)
XLA Modules:
  0.0 542.0 jit_solution(8547324513521723715)
XLA Ops:
  6.7 1.2 dynamic-slice
  8.9 8.7 %all-reduce = f32[256]{0:T(256)S(1)} all-reduce(f32[256]{0:T(256)S(1)} %dynamic-update-slice), channel_id=2, replica_groups=mesh['section'=2,'req'=4,'head'=4] {'req'}, use_global_device_ids=true, to_apply=%add | all-reduce | flops 256 | bytes 2048
  17.8 10.1 %copy.112 = bf16[256,8,2,1280]{3,1,2,0:T(8,128)(2,1)} copy(bf16[256,8,2,1280]{3,2,1,0:T(2,128)(2,1)} %bitcast.237) | data formatting | bytes 20971520
  27.9 6.8 %fusion.50 = f32[64,2560]{1,0:T(8,128)} fusion(bf16[2048,2560]{1,0:T(8,128)(2,1)} %bitcast.228, f32[2048]{0:T(1024)S(1)} %bitcast.244, f32[64]{0:T(128)S(1)} %add_rsqrt_fusion.3, bf16[64,2048]{1,0:T(8,128)(2,1)S(1)} %copy-done, pred[]{:T(512)S(6)} %eq.72), kind=kOutput, calls=%fused_computation.95 | convolution fusion | flops 671744000 | bytes 11411713 | tf_op jit(solution)/shard_map/dot_general | solution.py:126
  34.8 15.4 %copy.168 = bf16[1,2,8192,2,256]{4,2,3,1,0:T(8,128)(2,1)} copy(bf16[1,2,8192,2,256]{4,3,2,1,0:T(2,128)(2,1)} %param.31) | data formatting | bytes 33554432 | tf_op args[8]
  50.6 1.9 copy.169
  52.9 9.7 %reduce-scatter.5.cloned.1.call-done = f32[16,2560]{1,0:T(8,128)} async-done(((f32[64,2560]{1,0:T(8,128)}), f32[16,2560]{1,0:T(8,128)}) %reduce-scatter.5.cloned.1.call-update) | async-done | bytes 163856 | tf_op jit(solution)/shard_map/reduce_scatter | solution.py:75
  63.8 6.0 %all-gather.10 = bf16[4,1,2048]{2,1,0:T(2,128)(2,1)S(1)} all-gather(bf16[1,1,2048]{2,1,0:T(2,128)(2,1)S(1)} %reshape.294), channel_id=1, replica_groups=mesh['section'=2,'req'=4,'head'=4] {'req'}, dimensions={0}, use_global_device_ids=true | all-gather | bytes 20480 | tf_op jit(solution)/shard_map/all_gather | solution.py:71
  69.9 5.7 %select_reduce_fusion.3 = (f32[2,2,8]{2,1,0:T(2,128)S(1)}, f32[2,2,8,8192]{3,2,1,0:T(8,128)S(1)}) fusion(pred[2,8192]{1,0:T(4,128)(4,1)S(1)} %iota_compare_fusion.1, bf16[2,8192,2,256]{3,1,2,0:T(8,128)(2,1)} %bitcast.232, bf16[1,2,16,128]{3,1,2,0:T(2,128)(2,1)S(1)} %maximum_bitcast_fusion), kind=kOutput, calls=%fused_computation.61 | convolution fusion | flops 67895264 | bytes 9461888 | tf_op jit(solution)/shard_map/jkhd,jpkd->jkhp/dot_general | solution.py:152
  75.6 4.7 fusion.12
  80.8 5.1 all-gather.1
  86.1 6.4 %all-gather.3 = f32[8,2,8,128]{3,2,1,0:T(8,128)S(1)} all-gather(f32[2,2,8,128]{3,2,1,0:T(8,128)S(1)} %fusion.12), channel_id=5, replica_groups=mesh['section'=2,'req'=4,'head'=4] {'req'}, dimensions={0}, use_global_device_ids=true | all-gather | bytes 81920 | tf_op jit(solution)/shard_map/all_gather | solution.py:19
  92.5 5.3 all-gather.2
  100.9 6.9 %all_gather.87 = bf16[64,2048]{1,0:T(8,128)(2,1)S(1)} all-gather(bf16[16,2048]{1,0:T(8,128)(2,1)S(1)} %bitcast.246), channel_id=1, replica_groups=mesh['section'=2,'req'=4,'head'=4] {'req'}, dimensions={0}, use_global_device_ids=true | all-gather | bytes 327680 | tf_op jit(solution)/shard_map/all_gather | solution.py:71
  107.8 5.8 %fusion.96 = f32[64,2048]{1,0:T(8,128)} fusion(bf16[64,2048]{1,0:T(8,128)(2,1)S(1)} %all_gather.87, bf16[2048,2048]{1,0:T(8,128)(2,1)} %bitcast.230), kind=kOutput, calls=%fused_computation.202 | convolution fusion | flops 536870912 | bytes 9175040 | tf_op jit(solution)/shard_map/dot_general | solution.py:228
  113.7 20.9 %copy.115 = bf16[256,8,2,3584]{3,1,2,0:T(8,128)(2,1)} copy(bf16[256,8,2,3584]{3,2,1,0:T(2,128)(2,1)} %bitcast.236) | data formatting | bytes 58720256
  134.6 26.3 %all-reduce.9.cloned.1.call-done = f32[64,2048]{1,0:T(8,128)} async-done(((f32[64,2048]{1,0:T(8,128)}), f32[64,2048]{1,0:T(8,128)}) %all-reduce.9.cloned.1.call-update) | async-done | bytes 524304 | tf_op jit(solution)/shard_map/psum | solution.py:84
  160.9 1.2 fusion.30
  162.4 8.1 %all-reduce.1 = f32[256]{0:T(256)S(1)} all-reduce(f32[256]{0:T(256)S(1)} %dynamic-update-slice.1), channel_id=6, replica_groups=mesh['section'=2,'req'=4,'head'=4] {'req'}, use_global_device_ids=true, to_apply=%add.1 | all-reduce | flops 256 | bytes 2048
  170.7 13.3 %fusion.48 = f32[64,7168]{1,0:T(8,128)} fusion(bf16[2048,7168]{1,0:T(8,128)(2,1)} %bitcast.226, bf16[64,2048]{1,0:T(8,128)(2,1)S(1)} %get-tuple-element.849, f32[2048]{0:T(1024)S(1)} %bitcast.250, f32[64]{0:T(128)S(1)} %add_rsqrt_fusion.2), kind=kOutput, calls=%fused_computation.94 | convolution fusion | flops 1879572480 | bytes 31465728 | tf_op jit(solution)/shard_map/dot_general | solution.py:236
  184.1 34.0 %reduce-scatter.7.cloned.1.call-done = f32[16,7168]{1,0:T(8,128)} async-done(((f32[64,7168]{1,0:T(8,128)}), f32[16,7168]{1,0:T(8,128)}) %reduce-scatter.7.cloned.1.call-update) | async-done | bytes 458768 | tf_op jit(solution)/shard_map/reduce_scatter | solution.py:75
  218.1 1.1 fusion.61
  219.2 7.7 %all_gather.90 = bf16[64,3584]{1,0:T(8,128)(2,1)S(1)} all-gather(bf16[16,3584]{1,0:T(8,128)(2,1)S(1)} %fusion.61), channel_id=1, replica_groups=mesh['section'=2,'req'=4,'head'=4] {'req'}, dimensions={0}, use_global_device_ids=true | all-gather | bytes 573440 | tf_op jit(solution)/shard_map/all_gather | solution.py:71
  226.9 8.7 %fusion.8 = f32[64,2048]{1,0:T(8,128)} fusion(bf16[64,3584]{1,0:T(8,128)(2,1)S(1)} %all_gather.90, bf16[1,3584,2048]{2,1,0:T(8,128)(2,1)} %param.29), kind=kOutput, calls=%fused_computation.23 | convolution fusion | flops 939524096 | bytes 15663104 | tf_op jit(solution)/shard_map/dot_general | solution.py:246
  235.7 39.4 %all-reduce.11.cloned.1.call-done = f32[64,2048]{1,0:T(8,128)} async-done(((f32[64,2048]{1,0:T(8,128)}), f32[64,2048]{1,0:T(8,128)}) %all-reduce.11.cloned.1.call-update) | async-done | bytes 524304 | tf_op jit(solution)/shard_map/psum | solution.py:84
  276.2 1.3 collective-permute-start
  277.5 2.7 collective-permute-done
  280.6 7.8 %all-reduce.2 = f32[256]{0:T(256)S(1)} all-reduce(f32[256]{0:T(256)S(1)} %dynamic-update-slice.2), channel_id=7, replica_groups=mesh['section'=2,'req'=4,'head'=4] {'req'}, use_global_device_ids=true, to_apply=%add.2 | all-reduce | flops 256 | bytes 2048
  288.6 6.8 %fusion.46 = f32[64,2560]{1,0:T(8,128)} fusion(bf16[2048,2560]{1,0:T(8,128)(2,1)} %bitcast.229, bf16[64,2048]{1,0:T(8,128)(2,1)S(1)} %get-tuple-element.847, f32[64]{0:T(128)S(1)} %add_rsqrt_fusion.1, f32[2048]{0:T(1024)S(1)} %bitcast.245), kind=kOutput, calls=%fused_computation.93 | convolution fusion | flops 671612928 | bytes 11411712 | tf_op jit(solution)/shard_map/dot_general | solution.py:126
  295.5 25.1 %reduce-scatter.9.cloned.1.call-done = f32[16,2560]{1,0:T(8,128)} async-done(((f32[64,2560]{1,0:T(8,128)}), f32[16,2560]{1,0:T(8,128)}) %reduce-scatter.9.cloned.1.call-update) | async-done | bytes 163856 | tf_op jit(solution)/shard_map/reduce_scatter | solution.py:75
  321.9 6.3 %all-gather.11 = bf16[4,1,2048]{2,1,0:T(2,128)(2,1)S(1)} all-gather(bf16[1,1,2048]{2,1,0:T(2,128)(2,1)S(1)} %reshape.296), channel_id=1, replica_groups=mesh['section'=2,'req'=4,'head'=4] {'req'}, dimensions={0}, use_global_device_ids=true | all-gather | bytes 20480 | tf_op jit(solution)/shard_map/all_gather | solution.py:71
  328.2 5.7 %select_reduce_fusion.2 = (f32[2,2,8]{2,1,0:T(2,128)S(1)}, f32[2,2,8,8192]{3,2,1,0:T(8,128)S(1)}) fusion(pred[2,8192]{1,0:T(4,128)(4,1)S(1)} %iota_compare_fusion.1, bf16[2,8192,2,256]{3,1,2,0:T(8,128)(2,1)} %bitcast.234, bf16[1,2,16,128]{3,1,2,0:T(2,128)(2,1)S(1)} %maximum_bitcast_fusion.1), kind=kOutput, calls=%fused_computation.58 | convolution fusion | flops 67895264 | bytes 9461888 | tf_op jit(solution)/shard_map/jkhd,jpkd->jkhp/dot_general | solution.py:152
  333.9 4.7 fusion.10
  339.1 5.1 all-gather.6
  344.4 6.4 %all-gather.8 = f32[8,2,8,128]{3,2,1,0:T(8,128)S(1)} all-gather(f32[2,2,8,128]{3,2,1,0:T(8,128)S(1)} %fusion.10), channel_id=10, replica_groups=mesh['section'=2,'req'=4,'head'=4] {'req'}, dimensions={0}, use_global_device_ids=true | all-gather | bytes 81920 | tf_op jit(solution)/shard_map/all_gather | solution.py:19
  350.8 5.1 all-gather.7
  359.0 7.1 %all_gather.100 = bf16[64,2048]{1,0:T(8,128)(2,1)S(1)} all-gather(bf16[16,2048]{1,0:T(8,128)(2,1)S(1)} %bitcast.247), channel_id=1, replica_groups=mesh['section'=2,'req'=4,'head'=4] {'req'}, dimensions={0}, use_global_device_ids=true | all-gather | bytes 327680 | tf_op jit(solution)/shard_map/all_gather | solution.py:71
  366.1 5.8 %fusion.97 = f32[64,2048]{1,0:T(8,128)} fusion(bf16[64,2048]{1,0:T(8,128)(2,1)S(1)} %all_gather.100, bf16[2048,2048]{1,0:T(8,128)(2,1)} %bitcast.231), kind=kOutput, calls=%fused_computation.203 | convolution fusion | flops 536870912 | bytes 9175040 | tf_op jit(solution)/shard_map/dot_general | solution.py:228
  372.0 47.1 %all-reduce.13.cloned.1.call-done = f32[64,2048]{1,0:T(8,128)} async-done(((f32[64,2048]{1,0:T(8,128)}), f32[64,2048]{1,0:T(8,128)}) %all-reduce.13.cloned.1.call-update) | async-done | bytes 524304 | tf_op jit(solution)/shard_map/psum | solution.py:84
  419.1 1.2 fusion.38
  420.6 8.1 %all-reduce.3 = f32[256]{0:T(256)S(1)} all-reduce(f32[256]{0:T(256)S(1)} %dynamic-update-slice.3), channel_id=11, replica_groups=mesh['section'=2,'req'=4,'head'=4] {'req'}, use_global_device_ids=true, to_apply=%add.3 | all-reduce | flops 256 | bytes 2048
  428.9 13.4 %fusion.44 = f32[64,7168]{1,0:T(8,128)} fusion(bf16[2048,7168]{1,0:T(8,128)(2,1)} %bitcast.227, bf16[64,2048]{1,0:T(8,128)(2,1)S(1)} %get-tuple-element.840, f32[64]{0:T(128)S(1)} %add_rsqrt_fusion, f32[2048]{0:T(1024)S(1)} %bitcast.251), kind=kOutput, calls=%fused_computation.92 | convolution fusion | flops 1879572480 | bytes 31465728 | tf_op jit(solution)/shard_map/dot_general | solution.py:236
  442.3 34.0 %reduce-scatter.11.cloned.1.call-done = f32[16,7168]{1,0:T(8,128)} async-done(((f32[64,7168]{1,0:T(8,128)}), f32[16,7168]{1,0:T(8,128)}) %reduce-scatter.11.cloned.1.call-update) | async-done | bytes 458768 | tf_op jit(solution)/shard_map/reduce_scatter | solution.py:75
  476.3 1.1 fusion.60
  477.4 7.7 %all_gather.103 = bf16[64,3584]{1,0:T(8,128)(2,1)S(1)} all-gather(bf16[16,3584]{1,0:T(8,128)(2,1)S(1)} %fusion.60), channel_id=1, replica_groups=mesh['section'=2,'req'=4,'head'=4] {'req'}, dimensions={0}, use_global_device_ids=true | all-gather | bytes 573440 | tf_op jit(solution)/shard_map/all_gather | solution.py:71
  485.1 8.7 %fusion.6 = f32[64,2048]{1,0:T(8,128)} fusion(bf16[64,3584]{1,0:T(8,128)(2,1)S(1)} %all_gather.103, bf16[1,3584,2048]{2,1,0:T(8,128)(2,1)} %param.29), kind=kOutput, calls=%fused_computation.21 | convolution fusion | flops 939524096 | bytes 15663104 | tf_op jit(solution)/shard_map/dot_general | solution.py:246
  493.9 39.5 %all-reduce.15.cloned.1.call-done = f32[64,2048]{1,0:T(8,128)} async-done(((f32[64,2048]{1,0:T(8,128)}), f32[64,2048]{1,0:T(8,128)}) %all-reduce.15.cloned.1.call-update) | async-done | bytes 524304 | tf_op jit(solution)/shard_map/psum | solution.py:84
  533.3 1.8 fusion.43
  (146 shorter events, 14.8 us)
Async XLA Ops:
  6.5 56.0 %reduce-scatter.5.cloned.1.call-start = ((), (), s32[]{:S(2)}) async-start(), calls=%async_computation.4 | async-start | bytes 819200 | tf_op jit(solution)/shard_map/reduce_scatter | solution.py:75
  17.7 10.1 %copy-start.1 = (bf16[1,2048]{1,0:T(2,128)(2,1)S(1)}, bf16[1,2048]{1,0:T(2,128)(2,1)}, u32[]{:S(2)}) copy-start(bf16[1,2048]{1,0:T(2,128)(2,1)} %param.24) | copy-start | bytes 12292
  17.8 10.1 %copy-start = (bf16[64,2048]{1,0:T(8,128)(2,1)S(1)}, bf16[64,2048]{1,0:T(8,128)(2,1)}, u32[]{:S(2)}) copy-start(bf16[64,2048]{1,0:T(8,128)(2,1)} %param.23) | copy-start | bytes 786436
  34.7 126.2 %all-reduce.9.cloned.1.call-start = ((), (), s32[]{:S(2)}) async-start(), calls=%async_computation.5 | async-start | bytes 1048576 | tf_op jit(solution)/shard_map/psum | solution.py:84
  34.8 15.4 %copy-start.3 = (s32[1,16]{1,0:T(1,128)S(1)}, s32[1,16]{1,0:T(1,128)}, u32[]{:S(2)}) copy-start(s32[1,16]{1,0:T(1,128)} %param.32) | copy-start | bytes 196
  50.5 2.2 copy-start.4
  113.6 104.5 %reduce-scatter.7.cloned.1.call-start = ((), (), s32[]{:S(2)}) async-start(), calls=%async_computation.6 | async-start | bytes 2293760 | tf_op jit(solution)/shard_map/reduce_scatter | solution.py:75
  113.6 20.9 %copy-start.2 = (bf16[1,2048]{1,0:T(2,128)(2,1)S(1)}, bf16[1,2048]{1,0:T(2,128)(2,1)}, u32[]{:S(2)}) copy-start(bf16[1,2048]{1,0:T(2,128)(2,1)} %param.27) | copy-start | bytes 12292
  184.0 91.1 %all-reduce.11.cloned.1.call-start = ((), (), s32[]{:S(2)}) async-start(), calls=%async_computation.7 | async-start | bytes 1048576 | tf_op jit(solution)/shard_map/psum | solution.py:84
  235.7 85.0 %reduce-scatter.9.cloned.1.call-start = ((), (), s32[]{:S(2)}) async-start(), calls=%async_computation.8 | async-start | bytes 819200 | tf_op jit(solution)/shard_map/reduce_scatter | solution.py:75
  276.2 4.0 collective-permute-start
  295.5 123.6 %all-reduce.13.cloned.1.call-start = ((), (), s32[]{:S(2)}) async-start(), calls=%async_computation.9 | async-start | bytes 1048576 | tf_op jit(solution)/shard_map/psum | solution.py:84
  371.9 104.3 %reduce-scatter.11.cloned.1.call-start = ((), (), s32[]{:S(2)}) async-start(), calls=%async_computation.10 | async-start | bytes 2293760 | tf_op jit(solution)/shard_map/reduce_scatter | solution.py:75
  442.2 91.1 %all-reduce.15.cloned.1.call-start = ((), (), s32[]{:S(2)}) async-start(), calls=%async_computation.11 | async-start | bytes 1048576 | tf_op jit(solution)/shard_map/psum | solution.py:84
Sparse Core Ops, SparseCore 0:
  34.8 27.6 reduce-scatter.4
  113.7 47.1 all-reduce.8
  184.2 33.8 reduce-scatter.6
  235.8 39.3 all-reduce.10
  295.6 25.0 reduce-scatter.8
  372.1 47.0 all-reduce.12
  442.4 33.8 reduce-scatter.10
  494.0 39.3 all-reduce.14
where the time goes:
time: 545 us; the launch traced here: 542 us
  waiting for transfers between devices  258 us (47%)
  blocking collectives  108 us (20%)
  matrix products  93.4 us (17%)
  local copies, waits for them, and re-layouts  53.2 us (10%)
  between operations  14.7 us (3%)
  other arithmetic  13.1 us (2%)
    psum x4, waiting for transfers between devices, head_total(): return lax.psum(values, 'head')  152 us
    reduce_scatter x4, waiting for transfers between devices, rows_project(): lax.psum_scatter(term_fn(jnp.int32(0), row_count * lax.axis_size('req')),...  103 us
    unnamed x27, local copies, waits for them, and re-layouts  50.6 us
    all_gather x6, blocking collectives, rows_apply(): lax.all_gather(values, 'req', axis=0, tiled=True)  41.7 us
    all_gather x6, blocking collectives, merged(): gathered = jax.tree.map(lambda a: lax.all_gather(a, axis), part)  33.5 us
    unnamed x4, blocking collectives  32.6 us
    dot_general x2, matrix products, ff_term(): return jnp.dot(normed_two, ff_weights, preferred_element_type=jnp.float32)  26.7 us
    dot_general x2, matrix products, project_hidden(): jnp.dot(piece_rows, lower_weights, preferred_element_type=jnp.float32)  17.5 us
  transfers between devices with their start and end apart: 9, of which 9 were waited for; matrix products, arithmetic and copies ran while one was open for 7% of the time, Pallas kernels for 0%

commit v1 on v0

--- a/solution.py
+++ b/solution.py
@@ -1,8 +1,11 @@
+import functools
 import math
 
 import jax
 import jax.numpy as jnp
 from jax import lax
+from jax.experimental import pallas as pl
+from jax.experimental.pallas import tpu as pltpu
 from jax.sharding import PartitionSpec as P
 
 MODEL_WIDTH = 8192
@@ -10,6 +13,13 @@
 KEY_VALUE_HEADS = 8
 HEAD_SIZE = 128
 LONG = 16384
+FF = 14336
+MOST_SLOTS = 256
+LANES = 128
+COLUMNS = 512
+VMEM_MEBIBYTES = 54
+FAR_SLOTS = 1024
+LOWEST = -1e30
 
 
 EPSILON = 1e-05
@@ -297,6 +307,558 @@
             incoming = shifted(output, "section", 1)
     return result.reshape(1, req_count * per_group, columns)
 
+def swap(value, axis, distance, section, target_section=None):
+    size = lax.axis_size(axis)
+    target_section = section if target_section is None else target_section
+    pairs = [(section * size + i, target_section * size + (i ^ distance)) for i in range(size)]
+    return lax.ppermute(value, ("section", axis), pairs)
+
+
+def gather_doubling(value, axis, section):
+    held, distance = value[None], 1
+    while distance < lax.axis_size(axis):
+        held = jnp.concatenate([held, swap(held, axis, distance, section)])
+        distance *= 2
+    return held
+
+
+def sum_doubling(value, axis, section):
+    distance = 1
+    while distance < lax.axis_size(axis):
+        other = swap(value, axis, distance, section)
+        total = value.astype(jnp.float32) + other.astype(jnp.float32)
+        distance *= 2
+        value = total.astype(jnp.bfloat16)
+    return total
+
+
+def exchange(values, axis):
+    return lax.all_to_all(values, axis, 0, 0)
+
+
+def in_vmem(count):
+    return [pl.BlockSpec(memory_space=pltpu.VMEM)] * count
+
+
+def in_hbm(count):
+    return [pl.BlockSpec(memory_space=pltpu.HBM)] * count
+
+
+def in_smem(count):
+    return [pl.BlockSpec(memory_space=pltpu.SMEM)] * count
+
+
+def params():
+    return pltpu.CompilerParams(vmem_limit_bytes=VMEM_MEBIBYTES * 2**20)
+
+
+def column_chunks(width):
+    return [(start, min(COLUMNS, width - start)) for start in range(0, width, COLUMNS)]
+
+
+def split_parts(value):
+    high = value.astype(jnp.bfloat16)
+    low = (value - high.astype(jnp.float32)).astype(jnp.bfloat16)
+    return high, low
+
+
+def sum_columns(values):
+    floats = values.astype(jnp.float32)
+    squares = jnp.sum(floats * floats, axis=-1, keepdims=True)
+    high, low = split_parts(squares)
+    lane = lax.broadcasted_iota(jnp.int32, (values.shape[0], LANES), 1)
+    return jnp.where(
+        lane == 0, high.astype(jnp.float32), jnp.where(lane == 1, low.astype(jnp.float32), 0.0)
+    )
+
+
+def row_scale(parts):
+    total = sum(jnp.sum(part.astype(jnp.float32), axis=-1, keepdims=True) for part in parts)
+    return lax.rsqrt(total / MODEL_WIDTH + EPSILON)
+
+
+def expand_rows(scaled, wide_ref):
+    rows, columns = scaled.shape
+    chunk = 2 * LANES
+    source = lax.broadcasted_iota(jnp.int32, (chunk, 2 * chunk), 0)
+    target = lax.broadcasted_iota(jnp.int32, (chunk, 2 * chunk), 1)
+    count = columns // chunk
+    stacked = jnp.concatenate([scaled[:, c * chunk : (c + 1) * chunk] for c in range(count)], 0)
+    for half in range(2):
+        select = jnp.where(target == 2 * source + half, 1.0, 0.0).astype(jnp.bfloat16)
+        spread = jnp.dot(stacked, select, preferred_element_type=jnp.float32).astype(jnp.bfloat16)
+        for c in range(count):
+            wide_ref[half * rows : (half + 1) * rows, 2 * c * chunk : 2 * (c + 1) * chunk] = spread[
+                c * rows : (c + 1) * rows
+            ]
+
+
+def scale_columns(values, gain):
+    return (values.astype(jnp.float32) * gain.astype(jnp.float32)).astype(jnp.bfloat16)
+
+
+def start_pair_copies(weight_ref, weights, sems):
+    copies = []
+    for c, (start, width) in enumerate(column_chunks(weight_ref.shape[3])):
+        copies.append(
+            pltpu.make_async_copy(
+                weight_ref.at[0, :, :, pl.ds(start, width)],
+                weights.at[c, :, :, pl.ds(0, width)],
+                sems.at[c],
+            )
+        )
+    for copy in copies:
+        copy.start()
+    return copies
+
+
+def qkv_kernel(peers, inputs_ref, gain_ref, table_ref, weight_ref, out_ref, wide, weights, sems):
+    rows, depth = inputs_ref.shape
+    blocks = rows // peers
+    width = weight_ref.shape[3]
+    far = peers // 2 * blocks
+    copies = start_pair_copies(weight_ref, weights, sems)
+    expand_rows(scale_columns(inputs_ref[...], gain_ref[...]), wide)
+
+    def write(result, start, size, tail):
+        lanes = pl.ds(start, size)
+        long_rows = [result[r : r + 1] for r in (0, far, rows, rows + far)]
+        extra = jnp.concatenate(long_rows + tail, 0).astype(jnp.bfloat16)
+        for p in range(peers):
+            for k in range(2):
+                first = k * rows + p * blocks
+                out_ref[p, k * blocks : (k + 1) * blocks, lanes] = result[
+                    first : first + blocks
+                ].astype(jnp.bfloat16)
+            out_ref[p, 2 * blocks :, lanes] = extra
+
+    sums = sum_columns(inputs_ref[...])
+    high, low = split_parts(table_ref[0:1])
+    write(
+        jnp.concatenate([sums, sums], 0),
+        width,
+        LANES,
+        [high.astype(jnp.float32), low.astype(jnp.float32), jnp.zeros((blocks - 6, LANES), jnp.float32)],
+    )
+    for c, (start, size) in enumerate(column_chunks(width)):
+        copies[c].wait()
+        result = jnp.dot(
+            wide[...],
+            weights[c, :, :, 0:size].reshape(2 * depth, size),
+            preferred_element_type=jnp.float32,
+        )
+        write(result, start, size, [jnp.zeros((blocks - 4, size), jnp.float32)])
+
+
+def project_qkv(inputs, gain, table, weight, peers):
+    rows = inputs.shape[0]
+    depth, pair, width = weight.shape[1:]
+    chunks = len(column_chunks(width))
+    return pl.pallas_call(
+        functools.partial(qkv_kernel, peers),
+        out_shape=jax.ShapeDtypeStruct((peers, 3 * rows // peers, width + LANES), jnp.bfloat16),
+        in_specs=in_vmem(3) + in_hbm(1),
+        out_specs=pl.BlockSpec(memory_space=pltpu.VMEM),
+        scratch_shapes=[
+            pltpu.VMEM((pair * rows, pair * depth), jnp.bfloat16),
+            pltpu.VMEM((chunks, depth, pair, COLUMNS), jnp.bfloat16),
+            pltpu.SemaphoreType.DMA((chunks,)),
+        ],
+        compiler_params=params(),
+        name="project_qkv",
+    )(inputs, gain, table, weight)
+
+
+def attention_kernel(peers, *refs):
+    pieces_ref, table_ref, starts, lengths, split, packed_ref, long_ref, out_ref = refs[:8]
+    piece_refs = [pieces_ref.at[p] for p in range(peers)]
+    (rope, packed, far, queries, keys, values, scores, far_scores, merged_rows, packed_sem, far_sems) = (
+        refs[8:]
+    )
+    group = lax.axis_index("req")
+    blocks = out_ref.shape[0] // 2
+    heads = QUERY_HEADS // KEY_VALUE_HEADS
+    pairs = 2 * heads
+    window = scores.shape[2] // 2
+    slots = packed.shape[0]
+    far_chunks = far.shape[1] // FAR_SLOTS
+    scale = 1.0 / math.sqrt(HEAD_SIZE)
+    live = [split[0, 0], split[1, 0]]
+
+    def far_copy(j, c):
+        return pltpu.make_async_copy(
+            long_ref.at[0, j, pl.ds(c * FAR_SLOTS, FAR_SLOTS)],
+            far.at[j, pl.ds(c * FAR_SLOTS, FAR_SLOTS)],
+            far_sems.at[j, c],
+        )
+
+    packed_copy = pltpu.make_async_copy(packed_ref.at[0], packed, packed_sem)
+    packed_copy.start()
+    for j in range(2):
+        for c in range(far_chunks):
+
+            @pl.when(c * FAR_SLOTS < live[j])
+            def _():
+                far_copy(j, c).start()
+
+    width = HEAD_SIZE * (heads + 2)
+    scale_rows = row_scale([piece[:, width:] for piece in piece_refs])
+    far_tables = [
+        sum(
+            pieces_ref[j * (peers // 2), 2 * blocks :, width:][row : row + 1].astype(jnp.float32)
+            for row in (4, 5)
+        )
+        for j in range(2)
+    ]
+    own_table = table_ref[...]
+    table = jnp.concatenate(
+        [own_table, own_table] + far_tables * 2 + [jnp.zeros((blocks - 4, HEAD_SIZE), jnp.float32)], 0
+    )
+    turned = pltpu.roll(table, HEAD_SIZE // 2, 1)
+    lower = lax.broadcasted_iota(jnp.int32, table.shape, 1) < HEAD_SIZE // 2
+    cosine = jnp.where(lower, table, turned)
+    sine = jnp.where(lower, -turned, table)
+    for b in range(heads + 2):
+        lanes = slice(b * HEAD_SIZE, (b + 1) * HEAD_SIZE)
+        block = sum(piece[:, lanes].astype(jnp.float32) for piece in piece_refs) * scale_rows
+        if b <= heads:
+            block = block * cosine + pltpu.roll(block, HEAD_SIZE // 2, 1) * sine
+        block = block.astype(jnp.bfloat16).astype(jnp.float32)
+        rope[:, lanes] = block
+        for k in range(2):
+            own_rows = block[k * blocks : (k + 1) * blocks]
+            if b < heads:
+                queries[:, k * heads + b, :] = own_rows
+            else:
+                for h in range(heads):
+                    (keys if b == heads else values)[:, k * heads + h, :] = own_rows
+
+    def same_head(columns):
+        row = lax.broadcasted_iota(jnp.int32, (pairs, columns), 0)
+        column = lax.broadcasted_iota(jnp.int32, (pairs, columns), 1)
+        return (row // heads) == (column % 2), column // 2
+
+    def contract(a, b):
+        return lax.dot_general(a, b, (((1,), (1,)), ((), ())), preferred_element_type=jnp.float32)
+
+    packed_copy.wait()
+    matching, slot = same_head(2 * window)
+    first_slots = []
+    for r in range(blocks):
+        first = jnp.minimum(starts[r], slots - window)
+        first_slots.append(first)
+        low = starts[r] - first
+        segment = packed[pl.ds(first, window), :, 0:HEAD_SIZE].reshape(2 * window, HEAD_SIZE)
+        own = contract(queries[r].astype(jnp.bfloat16), segment) * scale
+        inside = matching & (slot >= low) & (slot < low + lengths[r])
+        scores[r] = jnp.where(inside, own, LOWEST)
+    own_score = jnp.sum(queries[...] * keys[...], axis=-1, keepdims=True) * scale
+    row_max = jnp.maximum(jnp.max(scores[...], axis=-1, keepdims=True), own_score)
+    weights = jnp.exp(scores[...] - row_max).astype(jnp.bfloat16)
+    own_weight = jnp.exp(own_score - row_max).astype(jnp.bfloat16).astype(jnp.float32)
+    totals = jnp.sum(weights.astype(jnp.float32), axis=-1, keepdims=True) + own_weight
+    near_peak = row_max[0] + jnp.log(totals[0])
+    for r in range(blocks):
+        segment = packed[pl.ds(first_slots[r], window), :, HEAD_SIZE:].reshape(2 * window, HEAD_SIZE)
+        summed = jnp.dot(weights[r], segment, preferred_element_type=jnp.float32)
+        summed = summed + own_weight[r] * values[r]
+        merged_rows[r] = summed / totals[r]
+
+    matching, slot = same_head(2 * FAR_SLOTS)
+    for j in range(2):
+        long_rows = jnp.concatenate(
+            [
+                rope[2 * blocks + 2 * k + j : 2 * blocks + 2 * k + j + 1, h * HEAD_SIZE : (h + 1) * HEAD_SIZE]
+                for k in range(2)
+                for h in range(heads)
+            ],
+            0,
+        ).astype(jnp.bfloat16)
+        count = (live[j] + FAR_SLOTS - 1) // FAR_SLOTS
+
+        def score(c, peak):
+            far_copy(j, c).wait()
+            chunk = far[j, pl.ds(c * FAR_SLOTS, FAR_SLOTS), :, 0:HEAD_SIZE].reshape(
+                2 * FAR_SLOTS, HEAD_SIZE
+            )
+            found = contract(long_rows, chunk) * scale
+            found = jnp.where(matching & (slot < live[j] - c * FAR_SLOTS), found, LOWEST)
+            far_scores[c] = found
+            return jnp.maximum(peak, jnp.max(found, axis=-1, keepdims=True))
+
+        peak = lax.fori_loop(0, count, score, jnp.full((pairs, 1), LOWEST, jnp.float32))
+
+        def weigh(c, state):
+            total, summed = state
+            weight = jnp.exp(far_scores[c] - peak).astype(jnp.bfloat16)
+            chunk = far[j, pl.ds(c * FAR_SLOTS, FAR_SLOTS), :, HEAD_SIZE:].reshape(
+                2 * FAR_SLOTS, HEAD_SIZE
+            )
+            total = total + jnp.sum(weight.astype(jnp.float32), axis=-1, keepdims=True)
+            return total, summed + jnp.dot(weight, chunk, preferred_element_type=jnp.float32)
+
+        total, summed = lax.fori_loop(
+            0,
+            count,
+            weigh,
+            (jnp.zeros((pairs, 1), jnp.float32), jnp.zeros((pairs, HEAD_SIZE), jnp.float32)),
+        )
+        far_peak = peak + jnp.log(total)
+        result = summed / total
+        owner = group == j * (peers // 2)
+        top = jnp.maximum(far_peak, near_peak)
+        far_part = jnp.exp(far_peak - top)
+        near_part = jnp.exp(near_peak - top)
+        both = far_part + near_part
+        result = jnp.where(owner, (result * far_part + merged_rows[0] * near_part) / both, result)
+        log_total = jnp.where(owner, top + jnp.log(both), far_peak)
+        high, low = split_parts(log_total)
+        merged_rows[blocks + j] = result
+        merged_rows[blocks + 2 + j] = jnp.broadcast_to(high.astype(jnp.float32), result.shape)
+        merged_rows[blocks + 4 + j] = jnp.broadcast_to(low.astype(jnp.float32), result.shape)
+    merged_rows[blocks + 6 :] = jnp.zeros((blocks - 6, pairs, HEAD_SIZE), jnp.float32)
+    for b in range(pairs):
+        out_ref[:, b * HEAD_SIZE : (b + 1) * HEAD_SIZE] = merged_rows[:, b, :].astype(jnp.bfloat16)
+
+
+def attend(pieces, table, starts, lengths, split, packed_cache, long_cache):
+    peers = pieces.shape[0]
+    blocks = pieces.shape[1] // 3
+    heads = QUERY_HEADS // KEY_VALUE_HEADS
+    pairs = 2 * heads
+    slots = packed_cache.shape[1]
+    far_slots = long_cache.shape[2]
+    return pl.pallas_call(
+        functools.partial(attention_kernel, peers),
+        out_shape=jax.ShapeDtypeStruct((2 * blocks, pairs * HEAD_SIZE), jnp.bfloat16),
+        in_specs=in_vmem(2) + in_smem(3) + in_hbm(2),
+        out_specs=pl.BlockSpec(memory_space=pltpu.VMEM),
+        scratch_shapes=[
+            pltpu.VMEM((3 * blocks, (heads + 2) * HEAD_SIZE), jnp.float32),
+            pltpu.VMEM((slots, 2, 2 * HEAD_SIZE), jnp.bfloat16),
+            pltpu.VMEM((2, far_slots, 2, 2 * HEAD_SIZE), jnp.bfloat16),
+            pltpu.VMEM((blocks, pairs, HEAD_SIZE), jnp.float32),
+            pltpu.VMEM((blocks, pairs, HEAD_SIZE), jnp.float32),
+            pltpu.VMEM((blocks, pairs, HEAD_SIZE), jnp.float32),
+            pltpu.VMEM((blocks, pairs, 2 * MOST_SLOTS), jnp.float32),
+            pltpu.VMEM((far_slots // FAR_SLOTS, pairs, 2 * FAR_SLOTS), jnp.float32),
+            pltpu.VMEM((2 * blocks, pairs, HEAD_SIZE), jnp.float32),
+            pltpu.SemaphoreType.DMA,
+            pltpu.SemaphoreType.DMA((2, far_slots // FAR_SLOTS)),
+        ],
+        compiler_params=params(),
+        name="attend",
+    )(pieces, table, starts, lengths, split, packed_cache, long_cache)
+
+
+def start_column_copies(weight_at, weights, sems):
+    copies = []
+    for c, (start, width) in enumerate(column_chunks(weight_at.shape[1])):
+        copies.append(
+            pltpu.make_async_copy(weight_at.at[:, pl.ds(start, width)], weights.at[c], sems.at[c])
+        )
+    for copy in copies:
+        copy.start()
+    return copies
+
+
+def multiply_columns(rows_ref, weights, copies, out_ref):
+    for c, copy in enumerate(copies):
+        copy.wait()
+        out_ref[:, c * COLUMNS : (c + 1) * COLUMNS] = jnp.dot(
+            rows_ref[...], weights[c], preferred_element_type=jnp.float32
+        ).astype(out_ref.dtype)
+
+
+def output_kernel(pieces_ref, weight_ref, out_ref, whole, weights, sems):
+    peers = pieces_ref.shape[0]
+    group = lax.axis_index("req")
+    blocks = pieces_ref.shape[1] // 2
+    copies = start_column_copies(weight_ref, weights, sems)
+    for d in range(peers):
+        start = pl.multiple_of(lax.bitwise_xor(group, d) * blocks, blocks)
+        whole[pl.ds(start, blocks)] = pieces_ref[d, 0:blocks]
+    extras = [pieces_ref[d, blocks:].astype(jnp.float32) for d in range(peers)]
+    for j in range(2):
+        peaks = [e[2 + j : 3 + j] + e[4 + j : 5 + j] for e in extras]
+        top = functools.reduce(jnp.maximum, peaks)
+        parts = [jnp.exp(peak - top) for peak in peaks]
+        merged_row = sum(e[j : j + 1] * part for e, part in zip(extras, parts)) / sum(parts)
+        rows = slice(j * (peers // 2) * blocks, j * (peers // 2) * blocks + blocks)
+        row = lax.broadcasted_iota(jnp.int32, (blocks, whole.shape[1]), 0)
+        whole[rows] = jnp.where(
+            row == 0, merged_row, whole[rows].astype(jnp.float32)
+        ).astype(jnp.bfloat16)
+    multiply_columns(whole, weights, copies, out_ref)
+
+
+def project_columns(kernel, pieces, weight, rows, depth, width, name):
+    chunks = len(column_chunks(width))
+    return pl.pallas_call(
+        kernel,
+        out_shape=jax.ShapeDtypeStruct((rows, width), jnp.bfloat16),
+        in_specs=in_vmem(1) + in_hbm(1),
+        out_specs=pl.BlockSpec(memory_space=pltpu.VMEM),
+        scratch_shapes=[
+            pltpu.VMEM((rows, depth), jnp.bfloat16),
+            pltpu.VMEM((chunks, depth, COLUMNS), jnp.bfloat16),
+            pltpu.SemaphoreType.DMA((chunks,)),
+        ],
+        compiler_params=params(),
+        name=name,
+    )(pieces, weight)
+
+
+def project_output(pieces, weight):
+    rows = pieces.shape[0] * pieces.shape[1] // 2
+    return project_columns(output_kernel, pieces, weight, rows, *weight.shape, "project_output")
+
+
+def down_kernel(pieces_ref, weight_ref, out_ref, whole, weights, sems):
+    peers, _, width = pieces_ref.shape
+    group = lax.axis_index("req")
+    copies = start_column_copies(weight_ref.at[0], weights, sems)
+    for d in range(peers):
+        start = pl.multiple_of(lax.bitwise_xor(group, d) * width, LANES)
+        whole[:, pl.ds(start, width)] = pieces_ref[d]
+    multiply_columns(whole, weights, copies, out_ref)
+
+
+def project_down(pieces, weight):
+    return project_columns(down_kernel, pieces, weight, pieces.shape[1], *weight.shape[1:], "project_down")
+
+
+def gate_up_kernel(peers, inputs_ref, gain_ref, weight_ref, out_ref, wide, weights, total, sems):
+    rows, depth = inputs_ref.shape
+    copies = start_pair_copies(weight_ref, weights, sems)
+    expand_rows(scale_columns(inputs_ref[...], gain_ref[...]), wide)
+    sums = sum_columns(inputs_ref[...]).astype(jnp.bfloat16)
+    width = total.shape[1] // peers
+    for p in range(peers):
+        out_ref[p, 0:rows, width:] = sums
+        out_ref[p, rows:, width:] = sums
+    done = 0
+    for c, copy in enumerate(copies):
+        copy.wait()
+        total[:, c * COLUMNS : (c + 1) * COLUMNS] = jnp.dot(
+            wide[...],
+            weights[c].reshape(2 * depth, COLUMNS),
+            preferred_element_type=jnp.float32,
+        ).astype(jnp.bfloat16)
+        while done < peers and (done + 1) * width <= (c + 1) * COLUMNS:
+            out_ref[done, :, 0:width] = total[:, done * width : (done + 1) * width]
+            done += 1
+
+
+def project_gate_up(inputs, gain, weight, peers):
+    rows = inputs.shape[0]
+    depth, pair, width = weight.shape[1:]
+    chunks = len(column_chunks(width))
+    return pl.pallas_call(
+        functools.partial(gate_up_kernel, peers),
+        out_shape=jax.ShapeDtypeStruct((peers, pair * rows, width // peers + LANES), jnp.bfloat16),
+        in_specs=in_vmem(2) + in_hbm(1),
+        out_specs=pl.BlockSpec(memory_space=pltpu.VMEM),
+        scratch_shapes=[
+            pltpu.VMEM((pair * rows, pair * depth), jnp.bfloat16),
+            pltpu.VMEM((chunks, depth, pair, COLUMNS), jnp.bfloat16),
+            pltpu.VMEM((pair * rows, width), jnp.bfloat16),
+            pltpu.SemaphoreType.DMA((chunks,)),
+        ],
+        compiler_params=params(),
+        name="project_gate_up",
+    )(inputs, gain, weight)
+
+
+def hidden_kernel(pieces_ref, out_ref):
+    peers = pieces_ref.shape[0]
+    rows, width = out_ref.shape
+    factor = row_scale([pieces_ref[p, 0:rows, width:] for p in range(peers)])
+
+    def summed(first):
+        return sum(
+            pieces_ref[p, first : first + rows, 0:width].astype(jnp.float32) for p in range(peers)
+        ) * factor
+
+    gate, up = summed(0), summed(rows)
+    out_ref[...] = (gate / (1.0 + jnp.exp(-gate)) * up).astype(jnp.bfloat16)
+
+
+def gated_units(pieces):
+    rows, width = pieces.shape[1] // 2, pieces.shape[2] - LANES
+    return pl.pallas_call(
+        hidden_kernel,
+        out_shape=jax.ShapeDtypeStruct((rows, width), jnp.bfloat16),
+        in_specs=in_vmem(1),
+        out_specs=pl.BlockSpec(memory_space=pltpu.VMEM),
+        compiler_params=params(),
+        name="gated_units",
+    )(pieces)
+
+
+def fast_layer(section, inputs, attention_gain, query_key_value_weight, head_output_weight, feedforward_gain, gate_up, down_weight, packed_cache, long_cache, table, *segments):
+    req_count = lax.axis_size("req")
+    terms = project_qkv(inputs, attention_gain, table, query_key_value_weight, req_count)
+    own = attend(exchange(terms, "req"), table, *segments, packed_cache, long_cache)
+    out_weight = head_output_weight.reshape(-1, head_output_weight.shape[3])
+    attended = project_output(gather_doubling(own, "req", section), out_weight)
+    attended = sum_doubling(attended, "head", section)
+    residual = (inputs.astype(jnp.float32) + attended).astype(jnp.bfloat16)
+    terms = project_gate_up(residual, feedforward_gain, gate_up, req_count)
+    hidden = gated_units(exchange(terms, "req"))
+    lowered = project_down(gather_doubling(hidden, "req", section), down_weight)
+    lowered = sum_doubling(lowered, "head", section)
+    return (residual.astype(jnp.float32) + lowered).astype(jnp.bfloat16)
+
+
+def rope_table(lengths):
+    req_count, group = lax.axis_size("req"), lax.axis_index("req")
+    owner = (group == 0) | (group == req_count // 2)
+    long_row = (jnp.arange(lengths.shape[1]) == 0) & owner
+    position = lengths[0] + jnp.where(long_row, LONG, 0).astype(jnp.int32)
+    half_dim = HEAD_SIZE // 2
+    inverse = 1.0 / 10000.0 ** (jnp.arange(half_dim).astype(jnp.float32) * 2.0 / HEAD_SIZE)
+    angles = position.astype(jnp.float32)[:, None] * inverse[None, :]
+    return jnp.concatenate([jnp.cos(angles), jnp.sin(angles)], 1)
+
+
+def fast_local(tokens, attention_gain, query_key_value_weight, head_output_weight, feedforward_gain, gate_up, down_weight, packed_cache, long_cache, lengths, long_split):
+    layer_arrays = (
+        attention_gain,
+        query_key_value_weight,
+        head_output_weight,
+        feedforward_gain,
+        gate_up,
+        down_weight,
+        packed_cache,
+        long_cache,
+        rope_table(lengths),
+        jnp.cumsum(lengths[0]) - lengths[0],
+        lengths[0],
+        long_split,
+    )
+    first = fast_layer(0, tokens, *layer_arrays)
+    second = fast_layer(1, swap(first, "head", 0, 0, 1), *layer_arrays)
+    return jnp.where(lax.axis_index("section") == 0, first, second)[None]
+
+
+def is_power_of_two(value):
+    return value & (value - 1) == 0
+
+
+def fits_fast(mesh):
+    req_count, head_count = mesh.shape["req"], mesh.shape["head"]
+    columns = MODEL_WIDTH // req_count
+    return (
+        mesh.shape["section"] == 2
+        and is_power_of_two(req_count)
+        and is_power_of_two(head_count)
+        and KEY_VALUE_HEADS == 2 * head_count
+        and columns % COLUMNS == 0
+        and FF % (head_count * COLUMNS) == 0
+        and FF % (head_count * req_count * LANES) == 0
+    )
+
 
 def solution(mesh):
     placed = (
@@ -313,5 +875,7 @@
         P(None, "req"),
     )
     return jax.shard_map(
-        local, mesh=mesh, in_specs=placed, out_specs=P("section", None, "req"), check_vma=False
-    )
+        fast_local if fits_fast(mesh) else local,
+        mesh=mesh,
+        in_specs=placed, out_specs=P("section", None, "req"), check_vma=False
+    )

time: 545 us -> 328 us (0.60)
  waiting for transfers between devices: 258 us -> 118 us
  Pallas kernels: 0 us -> 116 us
  matrix products: 93.4 us -> 0 us
  blocking collectives: 108 us -> 39.7 us
  local copies, waits for them, and re-layouts: 53.2 us -> 3.57 us
  starting transfers between devices: 1.59 us -> 30.4 us
  between operations: 14.7 us -> 0.37 us
  other arithmetic: 13.1 us -> 19.5 us
    psum x4 -> x0, waiting for transfers between devices: 152 us -> none  [head_total(): return lax.psum(values, 'head')]
    pallas_call x0 -> x12, Pallas kernels: none -> 116 us  [the longest x2 46.6 us: attend(): pl.pallas_call(functools.partial(attention_kernel, peers), out_shape=jax....]
    ppermute x1 -> x17, waiting for transfers between devices: 2.66 us -> 112 us  [swap(): return lax.ppermute(value, ('section', axis), pairs)]
    reduce_scatter x4 -> x0, waiting for transfers between devices: 103 us -> none  [rows_project(): lax.psum_scatter(term_fn(jnp.int32(0), row_count * lax.axis_size('req')),...]
    dot_general x18 -> x0, matrix products: 93.4 us -> none  [the longest x2 26.7 us: ff_term(): return jnp.dot(normed_two, ff_weights, preferred_element_type=jnp.float32)]
    all_gather x12 -> x0, blocking collectives: 75.2 us -> none  [the longest x6 41.7 us: rows_apply(): lax.all_gather(values, 'req', axis=0, tiled=True)]
    unnamed x27 -> x13, local copies, waits for them, and re-layouts: 50.6 us -> 2.83 us
    all_to_all x0 -> x3, blocking collectives: none -> 39.7 us  [exchange(): return lax.all_to_all(values, axis, 0, 0)]
  transfers between devices with their start and end apart: 9 -> 18, of which waited for: 9 -> 10; matrix products, arithmetic and copies ran while one was open for 7% -> 0% of each run, Pallas kernels for 0% -> 0%
where the time goes in v1:
time: 328 us; the launch traced here: 327 us
  waiting for transfers between devices  118 us (36%)
  Pallas kernels  116 us (35%)
  blocking collectives  39.7 us (12%)
  starting transfers between devices  30.4 us (9%)
  other arithmetic  19.5 us (6%)
  local copies, waits for them, and re-layouts  3.57 us (1%)
    ppermute x17, waiting for transfers between devices, swap(): return lax.ppermute(value, ('section', axis), pairs)  112 us
    pallas_call x2, Pallas kernels, attend(): pl.pallas_call(functools.partial(attention_kernel, peers), out_shape=jax....  46.6 us
    all_to_all x3, blocking collectives, exchange(): return lax.all_to_all(values, axis, 0, 0)  39.7 us
    pallas_call x4, Pallas kernels, project_columns(): pl.pallas_call(kernel, out_shape=jax.ShapeDtypeStruct((rows, width), jnp....  27.1 us
    ppermute x17, starting transfers between devices, swap(): return lax.ppermute(value, ('section', axis), pairs)  26.1 us
    pallas_call x2, Pallas kernels, project_gate_up(): pl.pallas_call(functools.partial(gate_up_kernel, peers), out_shape=jax.Sh...  24.5 us
    pallas_call x2, Pallas kernels, project_qkv(): pl.pallas_call(functools.partial(qkv_kernel, peers), out_shape=jax.ShapeD...  13.4 us
    concatenate x8, other arithmetic, gather_doubling(): held = jnp.concatenate([held, swap(held, axis, distance, section)])  10.7 us
  transfers between devices with their start and end apart: 18, of which 10 were waited for; matrix products, arithmetic and copies ran while one was open for 0% of the time, Pallas kernels for 0%

profile of v1, /device:TPU:1, one launch (start us, length us, event | category | flops | bytes accessed | tf_op | source)
XLA Modules:
  0.0 327.3 jit_solution(13108208711060535365)
XLA Ops:
  0.9 1.2 bitcast_subtract_fusion
  2.9 6.7 %project_qkv.2 = bf16[4,48,1408]{2,1,0:T(8,128)(2,1)} custom-call(bf16[64,2048]{1,0:T(8,128)(2,1)} %inputs_ref.1, bf16[1,2048]{1,0:T(2,128)(2,1)} %gain_ref.6, f32[16,128]{1,0:T(8,128)} %pad_maximum_fusion.8.table_ref.refs_1_, bf16[1,2048,2,1280]{3,2,1,0:T(2,128)(2,1)} %weight_ref.9), custom_call_target="tpu_custom_call" | custom-call | tf_op jit(solution)/shard_map/project_qkv/pallas_call | solution.py:457
  9.6 4.3 %all-to-all-start = ((bf16[4,48,1408]{2,1,0:T(8,128)(2,1)}), bf16[4,48,1408]{2,1,0:T(8,128)(2,1)S(1)}, u32[]{:S(2)}, u32[]{:S(2)}) async-start(bf16[4,48,1408]{2,1,0:T(8,128)(2,1)} %project_qkv.2), calls=%async_computation | async-start | bytes 1081344 | tf_op jit(solution)/shard_map/all_to_all | solution.py:336
  13.9 1.3 copy.16.refs_4_
  15.2 6.0 %all-to-all-done.refs_0_ = bf16[4,48,1408]{2,1,0:T(8,128)(2,1)S(1)} async-done(((bf16[4,48,1408]{2,1,0:T(8,128)(2,1)}), bf16[4,48,1408]{2,1,0:T(8,128)(2,1)S(1)}, u32[]{:S(2)}, u32[]{:S(2)}) %all-to-all-start) | async-done | bytes 540704 | tf_op jit(solution)/shard_map/all_to_all | solution.py:336
  22.0 23.3 %attend.2 = bf16[32,2048]{1,0:T(8,128)(2,1)} custom-call(bf16[4,48,1408]{2,1,0:T(8,128)(2,1)} %copy-done.2, f32[16,128]{1,0:T(8,128)} %pad_maximum_fusion.8.table_ref.refs_1_, s32[16]{0:T(128)} %get-tuple-element.7.refs_2_, s32[16]{0:T(128)} %bitcast.26, s32[2,1]{1,0:T(2,128)} %copy.16.refs_4_, bf16[1,2048,2,256]{3,2,1,0:T(2,128)(2,1)} %refs_5_.3, ...), custom_call_target="tpu_custom_call" | custom-call | tf_op jit(solution)/shard_map/attend/pallas_call | solution.py:631
  46.1 0.9 pad_maximum_fusion.4
  47.7 1.8 pad_maximum_fusion.pieces_ref
  49.5 5.8 %project_output.2 = bf16[64,2048]{1,0:T(8,128)(2,1)} custom-call(bf16[4,32,2048]{2,1,0:T(8,128)(2,1)} %pad_maximum_fusion.pieces_ref, bf16[2048,2048]{1,0:T(8,128)(2,1)} %bitcast.11), custom_call_target="tpu_custom_call" | custom-call | tf_op jit(solution)/shard_map/project_output/pallas_call | solution.py:697
  55.9 1.0 add_convert_fusion.7
  58.6 12.3 %project_gate_up.2 = bf16[4,128,1024]{2,1,0:T(8,128)(2,1)} custom-call(bf16[64,2048]{1,0:T(8,128)(2,1)} %add_convert_fusion.6.inputs_ref, bf16[1,2048]{1,0:T(2,128)(2,1)} %gain_ref.7, bf16[1,2048,2,3584]{3,2,1,0:T(2,128)(2,1)} %weight_ref.10), custom_call_target="tpu_custom_call" | custom-call | tf_op jit(solution)/shard_map/project_gate_up/pallas_call | solution.py:757
  70.9 13.2 %all_to_all.20.pieces_ref = bf16[4,128,1024]{2,1,0:T(8,128)(2,1)} all-to-all(bf16[4,128,1024]{2,1,0:T(8,128)(2,1)} %project_gate_up.2), channel_id=1, replica_groups=mesh['section'=2,'req'=4,'head'=4] {'req'}, dimensions={0} | all-to-all | bytes 2097152 | tf_op jit(solution)/shard_map/all_to_all | solution.py:336
  84.2 2.2 gated_units.2
  87.0 0.9 pad_maximum_fusion.6
  88.6 1.7 pad_maximum_fusion.2.pieces_ref
  90.3 7.8 %project_down.2 = bf16[64,2048]{1,0:T(8,128)(2,1)} custom-call(bf16[4,64,896]{2,1,0:T(8,128)(2,1)} %pad_maximum_fusion.2.pieces_ref, bf16[1,3584,2048]{2,1,0:T(8,128)(2,1)} %weight_ref.11), custom_call_target="tpu_custom_call" | custom-call | tf_op jit(solution)/shard_map/project_down/pallas_call | solution.py:697
  98.8 1.0 add_convert_fusion.5
  100.7 1.3 collective-permute-start.8
  102.0 69.3 %collective-permute-done.8.inputs_ref = bf16[64,2048]{1,0:T(8,128)(2,1)S(1)} collective-permute-done((bf16[64,2048]{1,0:T(8,128)(2,1)S(1)}, bf16[64,2048]{1,0:T(8,128)(2,1)S(1)}, u32[]{:S(2)}, u32[]{:S(2)}) %collective-permute-start.8) | collective-permute-done | bytes 262176 | tf_op jit(solution)/shard_map/ppermute | solution.py:314
  172.0 6.7 %project_qkv.3 = bf16[4,48,1408]{2,1,0:T(8,128)(2,1)} custom-call(bf16[64,2048]{1,0:T(8,128)(2,1)} %copy-done.4, bf16[1,2048]{1,0:T(2,128)(2,1)} %gain_ref.6, f32[16,128]{1,0:T(8,128)} %pad_maximum_fusion.8.table_ref.refs_1_, bf16[1,2048,2,1280]{3,2,1,0:T(2,128)(2,1)} %weight_ref.9), custom_call_target="tpu_custom_call" | custom-call | tf_op jit(solution)/shard_map/project_qkv/pallas_call | solution.py:457
  178.7 13.2 %all_to_all.21.refs_0_ = bf16[4,48,1408]{2,1,0:T(8,128)(2,1)} all-to-all(bf16[4,48,1408]{2,1,0:T(8,128)(2,1)} %project_qkv.3), channel_id=1, replica_groups=mesh['section'=2,'req'=4,'head'=4] {'req'}, dimensions={0} | all-to-all | bytes 1081344 | tf_op jit(solution)/shard_map/all_to_all | solution.py:336
  191.8 23.3 %attend.3 = bf16[32,2048]{1,0:T(8,128)(2,1)} custom-call(bf16[4,48,1408]{2,1,0:T(8,128)(2,1)} %all_to_all.21.refs_0_, f32[16,128]{1,0:T(8,128)} %pad_maximum_fusion.8.table_ref.refs_1_, s32[16]{0:T(128)} %get-tuple-element.7.refs_2_, s32[16]{0:T(128)} %bitcast.27, s32[2,1]{1,0:T(2,128)} %copy.16.refs_4_, bf16[1,2048,2,256]{3,2,1,0:T(2,128)(2,1)} %refs_5_.3, ...), custom_call_target="tpu_custom_call" | custom-call | tf_op jit(solution)/shard_map/attend/pallas_call | solution.py:631
  215.2 1.9 collective-permute-start.9
  217.1 4.0 %collective-permute-done.9 = bf16[1,32,2048]{2,1,0:T(8,128)(2,1)S(1)} collective-permute-done((bf16[1,32,2048]{2,1,0:T(8,128)(2,1)}, bf16[1,32,2048]{2,1,0:T(8,128)(2,1)S(1)}, u32[]{:S(2)}, u32[]{:S(2)}) %collective-permute-start.9) | collective-permute-done | bytes 131104 | tf_op jit(solution)/shard_map/ppermute | solution.py:314
  221.1 0.9 pad_maximum_fusion.5
  222.0 1.9 collective-permute-start.10
  224.0 5.2 %collective-permute-done.10 = bf16[2,32,2048]{2,1,0:T(8,128)(2,1)S(1)} collective-permute-done((bf16[2,32,2048]{2,1,0:T(8,128)(2,1)S(1)}, bf16[2,32,2048]{2,1,0:T(8,128)(2,1)S(1)}, u32[]{:S(2)}, u32[]{:S(2)}) %collective-permute-start.10) | collective-permute-done | bytes 262176 | tf_op jit(solution)/shard_map/ppermute | solution.py:314
  229.1 1.8 pad_maximum_fusion.1.pieces_ref
  230.9 5.8 %project_output.3 = bf16[64,2048]{1,0:T(8,128)(2,1)} custom-call(bf16[4,32,2048]{2,1,0:T(8,128)(2,1)} %pad_maximum_fusion.1.pieces_ref, bf16[2048,2048]{1,0:T(8,128)(2,1)} %bitcast.12), custom_call_target="tpu_custom_call" | custom-call | tf_op jit(solution)/shard_map/project_output/pallas_call | solution.py:697
  236.7 1.9 collective-permute-start.11
  238.6 5.4 %collective-permute-done.11 = bf16[64,2048]{1,0:T(8,128)(2,1)S(1)} collective-permute-done((bf16[64,2048]{1,0:T(8,128)(2,1)}, bf16[64,2048]{1,0:T(8,128)(2,1)S(1)}, u32[]{:S(2)}, u32[]{:S(2)}) %collective-permute-start.11) | collective-permute-done | bytes 262176 | tf_op jit(solution)/shard_map/ppermute | solution.py:314
  244.0 1.0 add_convert_fusion.3
  245.0 3.4 %collective-permute-start.12 = (bf16[64,2048]{1,0:T(8,128)(2,1)S(1)}, bf16[64,2048]{1,0:T(8,128)(2,1)S(1)}, u32[]{:S(2)}, u32[]{:S(2)}) collective-permute-start(bf16[64,2048]{1,0:T(8,128)(2,1)S(1)} %add_convert_fusion.3), channel_id=1, source_target_pairs={{16,18},{17,19},{18,16},{19,17},{20,22},{21,23},{22,20},{23,21},{2... | collective-permute-start | bytes 786440 | tf_op jit(solution)/shard_map/ppermute | solution.py:314
  248.4 7.4 %collective-permute-done.12 = bf16[64,2048]{1,0:T(8,128)(2,1)S(1)} collective-permute-done((bf16[64,2048]{1,0:T(8,128)(2,1)S(1)}, bf16[64,2048]{1,0:T(8,128)(2,1)S(1)}, u32[]{:S(2)}, u32[]{:S(2)}) %collective-permute-start.12) | collective-permute-done | bytes 262176 | tf_op jit(solution)/shard_map/ppermute | solution.py:314
  256.7 12.3 %project_gate_up.3 = bf16[4,128,1024]{2,1,0:T(8,128)(2,1)} custom-call(bf16[64,2048]{1,0:T(8,128)(2,1)} %add_convert_fusion.2.inputs_ref, bf16[1,2048]{1,0:T(2,128)(2,1)} %gain_ref.7, bf16[1,2048,2,3584]{3,2,1,0:T(2,128)(2,1)} %weight_ref.10), custom_call_target="tpu_custom_call" | custom-call | tf_op jit(solution)/shard_map/project_gate_up/pallas_call | solution.py:757
  268.9 13.2 %all_to_all.22.pieces_ref = bf16[4,128,1024]{2,1,0:T(8,128)(2,1)} all-to-all(bf16[4,128,1024]{2,1,0:T(8,128)(2,1)} %project_gate_up.3), channel_id=1, replica_groups=mesh['section'=2,'req'=4,'head'=4] {'req'}, dimensions={0} | all-to-all | bytes 2097152 | tf_op jit(solution)/shard_map/all_to_all | solution.py:336
  282.2 2.2 gated_units.3
  284.3 2.5 collective-permute-start.13
  286.9 3.2 collective-permute-done.13
  291.0 2.5 collective-permute-start.14
  293.5 4.2 %collective-permute-done.14 = bf16[2,64,896]{2,1,0:T(8,128)(2,1)S(1)} collective-permute-done((bf16[2,64,896]{2,1,0:T(8,128)(2,1)S(1)}, bf16[2,64,896]{2,1,0:T(8,128)(2,1)S(1)}, u32[]{:S(2)}, u32[]{:S(2)}) %collective-permute-start.14) | collective-permute-done | bytes 229408 | tf_op jit(solution)/shard_map/ppermute | solution.py:314
  297.8 1.7 pad_maximum_fusion.3.pieces_ref
  299.5 7.8 %project_down.3 = bf16[64,2048]{1,0:T(8,128)(2,1)} custom-call(bf16[4,64,896]{2,1,0:T(8,128)(2,1)} %pad_maximum_fusion.3.pieces_ref, bf16[1,3584,2048]{2,1,0:T(8,128)(2,1)} %weight_ref.11), custom_call_target="tpu_custom_call" | custom-call | tf_op jit(solution)/shard_map/project_down/pallas_call | solution.py:697
  307.3 1.9 collective-permute-start.15
  309.2 5.4 %collective-permute-done.15 = bf16[64,2048]{1,0:T(8,128)(2,1)S(1)} collective-permute-done((bf16[64,2048]{1,0:T(8,128)(2,1)}, bf16[64,2048]{1,0:T(8,128)(2,1)S(1)}, u32[]{:S(2)}, u32[]{:S(2)}) %collective-permute-start.15) | collective-permute-done | bytes 262176 | tf_op jit(solution)/shard_map/ppermute | solution.py:314
  314.6 1.0 add_convert_fusion.1
  315.6 3.1 collective-permute-start.16
  318.8 7.7 %collective-permute-done.16 = bf16[64,2048]{1,0:T(8,128)(2,1)S(1)} collective-permute-done((bf16[64,2048]{1,0:T(8,128)(2,1)S(1)}, bf16[64,2048]{1,0:T(8,128)(2,1)S(1)}, u32[]{:S(2)}, u32[]{:S(2)}) %collective-permute-start.16) | collective-permute-done | bytes 262176 | tf_op jit(solution)/shard_map/ppermute | solution.py:314
  (39 shorter events, 12.3 us)
Async XLA Ops:
  9.6 11.6 %all-to-all-start = ((bf16[4,48,1408]{2,1,0:T(8,128)(2,1)}), bf16[4,48,1408]{2,1,0:T(8,128)(2,1)S(1)}, u32[]{:S(2)}, u32[]{:S(2)}) async-start(bf16[4,48,1408]{2,1,0:T(8,128)(2,1)} %project_qkv.2), calls=%async_computation | async-start | bytes 1081344 | tf_op jit(solution)/shard_map/all_to_all | solution.py:336
  21.2 0.8 copy-start.2
  22.0 35.8 %copy-start.3 = (bf16[64,2048]{1,0:T(8,128)(2,1)S(1)}, bf16[64,2048]{1,0:T(8,128)(2,1)}, u32[]{:S(2)}) copy-start(bf16[64,2048]{1,0:T(8,128)(2,1)} %inputs_ref.1) | copy-start | bytes 786436
  45.4 0.7 collective-permute-start
  47.0 0.7 collective-permute-start.1
  55.2 0.7 collective-permute-start.2
  57.0 0.9 collective-permute-start.3
  70.9 29.6 %copy-start.1 = (bf16[64,2048]{1,0:T(8,128)(2,1)S(1)}, bf16[64,2048]{1,0:T(8,128)(2,1)}, u32[]{:S(2)}) copy-start(bf16[64,2048]{1,0:T(8,128)(2,1)} %add_convert_fusion.6.inputs_ref) | copy-start | bytes 786436
  86.3 0.7 collective-permute-start.4
  87.9 0.7 collective-permute-start.5
  98.1 0.7 collective-permute-start.6
  99.9 0.7 collective-permute-start.7
  100.7 70.6 %collective-permute-start.8 = (bf16[64,2048]{1,0:T(8,128)(2,1)S(1)}, bf16[64,2048]{1,0:T(8,128)(2,1)S(1)}, u32[]{:S(2)}, u32[]{:S(2)}) collective-permute-start(bf16[64,2048]{1,0:T(8,128)(2,1)S(1)} %add_convert_fusion.4), channel_id=1, source_target_pairs={{0,16},{1,17},{2,18},{3,19},{4,20},{5,21},{6,22},{7,23},{8,24},{9,... | collective-permute-start | bytes 786440 | tf_op jit(solution)/shard_map/ppermute | solution.py:314
  171.3 0.7 copy-start.4
  191.8 64.0 %copy-start.5 = (bf16[64,2048]{1,0:T(8,128)(2,1)S(1)}, bf16[64,2048]{1,0:T(8,128)(2,1)}, u32[]{:S(2)}) copy-start(bf16[64,2048]{1,0:T(8,128)(2,1)} %copy-done.4) | copy-start | bytes 786436
  215.2 5.9 %collective-permute-start.9 = (bf16[1,32,2048]{2,1,0:T(8,128)(2,1)}, bf16[1,32,2048]{2,1,0:T(8,128)(2,1)S(1)}, u32[]{:S(2)}, u32[]{:S(2)}) collective-permute-start(bf16[1,32,2048]{2,1,0:T(8,128)(2,1)} %bitcast.13), channel_id=1, source_target_pairs={{16,20},{20,16},{24,28},{28,24},{17,21},{21,17},{25,29},{29,25},{1... | collective-permute-start | bytes 393224 | tf_op jit(solution)/shard_map/ppermute | solution.py:314
  222.0 7.1 %collective-permute-start.10 = (bf16[2,32,2048]{2,1,0:T(8,128)(2,1)S(1)}, bf16[2,32,2048]{2,1,0:T(8,128)(2,1)S(1)}, u32[]{:S(2)}, u32[]{:S(2)}) collective-permute-start(bf16[2,32,2048]{2,1,0:T(8,128)(2,1)S(1)} %pad_maximum_fusion.5), channel_id=1, source_target_pairs={{16,24},{20,28},{24,16},{28,20},{17,25},{21,29},{25,17},{29,21},{1... | collective-permute-start | bytes 786440 | tf_op jit(solution)/shard_map/ppermute | solution.py:314
  236.7 7.3 %collective-permute-start.11 = (bf16[64,2048]{1,0:T(8,128)(2,1)}, bf16[64,2048]{1,0:T(8,128)(2,1)S(1)}, u32[]{:S(2)}, u32[]{:S(2)}) collective-permute-start(bf16[64,2048]{1,0:T(8,128)(2,1)} %project_output.3), channel_id=1, source_target_pairs={{16,17},{17,16},{18,19},{19,18},{20,21},{21,20},{22,23},{23,22},{2... | collective-permute-start | bytes 786440 | tf_op jit(solution)/shard_map/ppermute | solution.py:314
  245.0 10.8 %collective-permute-start.12 = (bf16[64,2048]{1,0:T(8,128)(2,1)S(1)}, bf16[64,2048]{1,0:T(8,128)(2,1)S(1)}, u32[]{:S(2)}, u32[]{:S(2)}) collective-permute-start(bf16[64,2048]{1,0:T(8,128)(2,1)S(1)} %add_convert_fusion.3), channel_id=1, source_target_pairs={{16,18},{17,19},{18,16},{19,17},{20,22},{21,23},{22,20},{23,21},{2... | collective-permute-start | bytes 786440 | tf_op jit(solution)/shard_map/ppermute | solution.py:314
  268.9 57.5 %copy-start = (bf16[64,2048]{1,0:T(8,128)(2,1)S(1)}, bf16[64,2048]{1,0:T(8,128)(2,1)}, u32[]{:S(2)}) copy-start(bf16[64,2048]{1,0:T(8,128)(2,1)} %add_convert_fusion.2.inputs_ref) | copy-start | bytes 786436
  284.3 5.7 %collective-permute-start.13 = (bf16[1,64,896]{2,1,0:T(8,128)(2,1)}, bf16[1,64,896]{2,1,0:T(8,128)(2,1)S(1)}, u32[]{:S(2)}, u32[]{:S(2)}) collective-permute-start(bf16[1,64,896]{2,1,0:T(8,128)(2,1)} %bitcast.22), channel_id=1, source_target_pairs={{16,20},{20,16},{24,28},{28,24},{17,21},{21,17},{25,29},{29,25},{1... | collective-permute-start | bytes 344072 | tf_op jit(solution)/shard_map/ppermute | solution.py:314
  291.0 6.8 %collective-permute-start.14 = (bf16[2,64,896]{2,1,0:T(8,128)(2,1)S(1)}, bf16[2,64,896]{2,1,0:T(8,128)(2,1)S(1)}, u32[]{:S(2)}, u32[]{:S(2)}) collective-permute-start(bf16[2,64,896]{2,1,0:T(8,128)(2,1)S(1)} %pad_maximum_fusion.7), channel_id=1, source_target_pairs={{16,24},{20,28},{24,16},{28,20},{17,25},{21,29},{25,17},{29,21},{1... | collective-permute-start | bytes 688136 | tf_op jit(solution)/shard_map/ppermute | solution.py:314
  307.3 7.3 %collective-permute-start.15 = (bf16[64,2048]{1,0:T(8,128)(2,1)}, bf16[64,2048]{1,0:T(8,128)(2,1)S(1)}, u32[]{:S(2)}, u32[]{:S(2)}) collective-permute-start(bf16[64,2048]{1,0:T(8,128)(2,1)} %project_down.3), channel_id=1, source_target_pairs={{16,17},{17,16},{18,19},{19,18},{20,21},{21,20},{22,23},{23,22},{2... | collective-permute-start | bytes 786440 | tf_op jit(solution)/shard_map/ppermute | solution.py:314
  315.6 10.8 %collective-permute-start.16 = (bf16[64,2048]{1,0:T(8,128)(2,1)S(1)}, bf16[64,2048]{1,0:T(8,128)(2,1)S(1)}, u32[]{:S(2)}, u32[]{:S(2)}) collective-permute-start(bf16[64,2048]{1,0:T(8,128)(2,1)S(1)} %add_convert_fusion.1), channel_id=1, source_target_pairs={{16,18},{17,19},{18,16},{19,17},{20,22},{21,23},{22,20},{23,21},{2... | collective-permute-start | bytes 786440 | tf_op jit(solution)/shard_map/ppermute | solution.py:314
